TPU v7x, 32 devices: a whole 2x2x4 slice. The times are simulated.
32 devices in a mesh: blk: 8 (over z, y), span: 4 (over x, core).
Axes of the slice: x: 2, y: 2, z: 4, core: 2. Of those that a mesh axis runs over, the one named last changes fastest.
Arguments:
- stiffness: float32 [128, 128], P('span'), may hold values from -1 to 8, as said below
- mistune_table: float32 [8, 128], P(None, 'span'), may hold values from 0.2 to 2
- sector_class: int32 [8], P('blk'), may hold values from 0 to 7
- lumped_mass: float32 [8, 128], P('blk', 'span'), may hold values from 0.5 to 2
- near_faces: int32 [8, 32], P('blk'), may hold values from 0 to 127
- far_faces: int32 [8, 32], P('blk'), may hold values from 0 to 127
- contact_state: int32 [8, 32], P('blk'), may hold values 0 or 1
- displacement: float32 [8, 128, 128], P('blk', 'span'), may hold values from -6 to 6
- velocity: float32 [8, 128, 128], P('blk', 'span'), may hold values from -6 to 6
- acceleration: float32 [8, 128, 128], P('blk', 'span'), may hold values from -6 to 6
- load_steps: float32 [2, 8, 128, 128], P(None, 'blk', 'span'), may hold values from -6 to 6
Outputs:
- new_displacement: float32 [8, 128, 128], P('blk', 'span')
- new_velocity: float32 [8, 128, 128], P('blk', 'span')
- new_acceleration: float32 [8, 128, 128], P('blk', 'span')
Inputs may be any that keep to these rules, and one draw needn't show every extreme that they name: stiffness is symmetric.
All inputs are finite; a program needn't handle non-finite values. No bound on the sum of `contact_state` on one device may be relied on, other than what follows from the above.
Results may differ from a plain program's by a relative error of at most 0.0003.
Values sent between devices are 32-bit elements; how exact they have to be, the bound alone decides.
A program may use at most 64 MiB of HBM per device.

v0:
```python
import jax
import jax.numpy as jnp
from jax import lax
from jax.sharding import PartitionSpec as P

BND = 64
STEPS = 2
ITERS = 5


highest = lax.Precision.HIGHEST
stick_rate = 20.0
slip_rate = 0.5
cycle_rate = 4.0


def passed_along(block, axis, distance):
    devices = range(lax.axis_size(axis))
    route = [((i - distance) % len(devices), i) for i in devices]
    return lax.ppermute(block, axis, route)


def column_norm(vector):
    return lax.psum(jnp.sum(vector * vector, axis=(0, 1)), ("blk", "span"))


def shards(
    stiffness,
    mistune_table,
    sector_class,
    lumped_mass,
    near_faces,
    far_faces,
    contact_state,
    displacement,
    velocity,
    acceleration,
    load_steps,
):
    sectors_here, rows_here, columns = displacement.shape
    sector_width = stiffness.shape[1]
    offset = lax.axis_index("span") * rows_here
    prior_face, prior_state = passed_along((far_faces[-1], contact_state[-1]), "blk", 1)
    contact_rates = jnp.where(contact_state == 1, stick_rate, slip_rate).astype(jnp.float32)
    prior_rate = jnp.where(prior_state == 1, stick_rate, slip_rate).astype(jnp.float32)
    rate_in = jnp.concatenate([prior_rate[None], contact_rates[:-1]], 0)
    face_in = jnp.concatenate([prior_face[None], far_faces[:-1]], 0)
    left_index = jnp.arange(BND, dtype=jnp.int32)[None]
    right_index = left_index + (sector_width - BND)
    index_list = jnp.concatenate([left_index, right_index, near_faces, face_in], 1)
    face_count = near_faces.shape[1]
    row_ids = jnp.arange(rows_here, dtype=jnp.int32)
    placement_map = (index_list[:, :, None] - offset == row_ids[None, None, :]).astype(jnp.float32)
    class_ids = jnp.arange(mistune_table.shape[0], dtype=jnp.int32)
    class_map = (sector_class[:, None] == class_ids[None, :]).astype(jnp.float32)
    extra_diag = jnp.dot(class_map, mistune_table, precision=highest)
    mass_cols = lumped_mass[:, :, None]
    pick_rows = jax.vmap(lambda values, rows: values[rows])

    def stiff_op(vector):
        gathered = lax.all_gather(vector, "span", axis=1, tiled=True)
        product = jnp.einsum("rk,skc->src", stiffness, gathered, precision=highest)
        picked = pick_rows(gathered, index_list)
        left_values = picked[:, :BND]
        right_values = picked[:, BND : 2 * BND]
        near_values = picked[:, 2 * BND : 2 * BND + face_count]
        far_values = picked[:, 2 * BND + face_count :]
        prior_right, prior_near = passed_along((right_values[-1], near_values[-1]), "blk", 1)
        next_left, next_far = passed_along((left_values[0], far_values[0]), "blk", -1)
        after_left = jnp.concatenate([left_values[1:], next_left[None]], 0)
        before_right = jnp.concatenate([prior_right[None], right_values[:-1]], 0)
        after_far = jnp.concatenate([far_values[1:], next_far[None]], 0)
        before_near = jnp.concatenate([prior_near[None], near_values[:-1]], 0)
        force_left = cycle_rate * (left_values - before_right)
        force_right = cycle_rate * (right_values - after_left)
        force_out = contact_rates[:, :, None] * (near_values - after_far)
        force_in = -rate_in[:, :, None] * (before_near - far_values)
        weights = jnp.concatenate([force_left, force_right, force_out, force_in], 1)
        spread = jnp.einsum("sir,sic->src", placement_map, weights, precision=highest)
        return product + extra_diag[:, :, None] * vector + spread

    for newmark_step in range(STEPS):
        predicted = displacement + velocity + 0.25 * acceleration
        residual = (
            load_steps[newmark_step]
            - mass_cols * acceleration
            - stiff_op(predicted + 0.25 * acceleration)
        )
        solution = acceleration
        direction = residual
        norm_now = column_norm(residual)
        for iteration in range(ITERS):
            image = mass_cols * direction + 0.25 * stiff_op(direction)
            curve = lax.psum(jnp.sum(direction * image, axis=(0, 1)), ("blk", "span"))
            step_length = norm_now / curve
            solution = solution + step_length * direction
            residual = residual - step_length * image
            norm_next = column_norm(residual)
            direction = residual + norm_next / norm_now * direction
            norm_now = norm_next
        displacement = predicted + 0.25 * solution
        velocity = velocity + 0.5 * (acceleration + solution)
        acceleration = solution
    return (displacement, velocity, acceleration)


def solution(mesh):
    placed = (
        P("span", None),
        P(None, "span"),
        P("blk"),
        P("blk", "span"),
        P("blk", None),
        P("blk", None),
        P("blk", None),
        P("blk", "span", None),
        P("blk", "span", None),
        P("blk", "span", None),
        P(None, "blk", "span", None),
    )
    return jax.shard_map(
        shards,
        mesh=mesh,
        in_specs=placed,
        out_specs=(P("blk", "span", None), P("blk", "span", None), P("blk", "span", None)),
        check_vma=False,
    )
```

profile of v0, /device:TPU:0, one launch (start us, length us, event | category | flops | bytes accessed | tf_op | source)
XLA Modules:
  0.0 977.4 jit_solution(5362765190922075942)
XLA Ops:
  7.9 5.2 all_gather.36
  30.7 5.2 all_gather.37
  42.2 5.0 collective-permute-done.6
  51.3 38.1 %all-reduce.1 = (f32[128]{0:T(128)S(1)}, f32[128]{0:T(128)S(1)}) all-reduce(f32[128]{0:T(128)S(1)} %get-tuple-element.6, f32[128]{0:T(128)S(1)} %get-tuple-element.5), channel_id=1, replica_groups=mesh['blk'=8,'span'=4] {'blk','span'}, use_global_device_ids=true, to_apply=%region_1.2 | all-reduce | flops 256 | bytes 2048 | tf_op jit(solution)/shard_map/psum | solution.py:24
  89.4 41.2 %psum.142 = f32[128]{0:T(128)S(1)} all-reduce(f32[128]{0:T(128)S(1)} %multiply_reduce_fusion.15), channel_id=1, replica_groups=mesh['blk'=8,'span'=4] {'blk','span'}, use_global_device_ids=true, to_apply=%region_5.6 | all-reduce | flops 128 | bytes 1024 | tf_op jit(solution)/shard_map/psum | solution.py:24
  130.6 5.5 all_gather.38
  152.1 38.1 %psum.143 = f32[128]{0:T(128)S(1)} all-reduce(f32[128]{0:T(128)S(1)} %get-tuple-element.72), channel_id=1, replica_groups=mesh['blk'=8,'span'=4] {'blk','span'}, use_global_device_ids=true, to_apply=%region_7.8 | all-reduce | flops 128 | bytes 1024 | tf_op jit(solution)/shard_map/psum | solution.py:94
  190.2 41.2 %psum.144 = f32[128]{0:T(128)S(1)} all-reduce(f32[128]{0:T(128)S(1)} %get-tuple-element.21), channel_id=1, replica_groups=mesh['blk'=8,'span'=4] {'blk','span'}, use_global_device_ids=true, to_apply=%region_9.10 | all-reduce | flops 128 | bytes 1024 | tf_op jit(solution)/shard_map/psum | solution.py:24
  231.4 5.5 all_gather.39
  252.8 38.3 %psum.145 = f32[128]{0:T(128)S(1)} all-reduce(f32[128]{0:T(128)S(1)} %get-tuple-element.74), channel_id=1, replica_groups=mesh['blk'=8,'span'=4] {'blk','span'}, use_global_device_ids=true, to_apply=%region_11.12 | all-reduce | flops 128 | bytes 1024 | tf_op jit(solution)/shard_map/psum | solution.py:94
  291.1 41.2 %psum.146 = f32[128]{0:T(128)S(1)} all-reduce(f32[128]{0:T(128)S(1)} %get-tuple-element.19), channel_id=1, replica_groups=mesh['blk'=8,'span'=4] {'blk','span'}, use_global_device_ids=true, to_apply=%region_13.14 | all-reduce | flops 128 | bytes 1024 | tf_op jit(solution)/shard_map/psum | solution.py:24
  332.3 5.5 all_gather.40
  353.7 38.1 %psum.147 = f32[128]{0:T(128)S(1)} all-reduce(f32[128]{0:T(128)S(1)} %get-tuple-element.76), channel_id=1, replica_groups=mesh['blk'=8,'span'=4] {'blk','span'}, use_global_device_ids=true, to_apply=%region_15.16 | all-reduce | flops 128 | bytes 1024 | tf_op jit(solution)/shard_map/psum | solution.py:94
  391.8 41.2 %psum.148 = f32[128]{0:T(128)S(1)} all-reduce(f32[128]{0:T(128)S(1)} %multiply_reduce_fusion.9), channel_id=1, replica_groups=mesh['blk'=8,'span'=4] {'blk','span'}, use_global_device_ids=true, to_apply=%region_17.18 | all-reduce | flops 128 | bytes 1024 | tf_op jit(solution)/shard_map/psum | solution.py:24
  433.0 5.5 all_gather.41
  454.5 38.1 %psum.149 = f32[128]{0:T(128)S(1)} all-reduce(f32[128]{0:T(128)S(1)} %fusion.48), channel_id=1, replica_groups=mesh['blk'=8,'span'=4] {'blk','span'}, use_global_device_ids=true, to_apply=%region_19.20 | all-reduce | flops 128 | bytes 1024 | tf_op jit(solution)/shard_map/psum | solution.py:94
  492.6 5.5 all_gather.42
  513.8 5.2 all_gather.43
  525.4 5.0 collective-permute-done.30
  534.5 37.8 %all-reduce = (f32[128]{0:T(128)S(1)}, f32[128]{0:T(128)S(1)}) all-reduce(f32[128]{0:T(128)S(1)} %get-tuple-element.4, f32[128]{0:T(128)S(1)} %get-tuple-element.3), channel_id=1, replica_groups=mesh['blk'=8,'span'=4] {'blk','span'}, use_global_device_ids=true, to_apply=%region_21.22 | all-reduce | flops 256 | bytes 2048 | tf_op jit(solution)/shard_map/psum | solution.py:24
  572.4 41.2 %psum.152 = f32[128]{0:T(128)S(1)} all-reduce(f32[128]{0:T(128)S(1)} %multiply_reduce_fusion.6), channel_id=1, replica_groups=mesh['blk'=8,'span'=4] {'blk','span'}, use_global_device_ids=true, to_apply=%region_25.26 | all-reduce | flops 128 | bytes 1024 | tf_op jit(solution)/shard_map/psum | solution.py:24
  613.5 5.5 all_gather.44
  635.5 37.6 %psum.153 = f32[128]{0:T(128)S(1)} all-reduce(f32[128]{0:T(128)S(1)} %get-tuple-element.79), channel_id=1, replica_groups=mesh['blk'=8,'span'=4] {'blk','span'}, use_global_device_ids=true, to_apply=%region_27.28 | all-reduce | flops 128 | bytes 1024 | tf_op jit(solution)/shard_map/psum | solution.py:94
  673.1 41.2 %psum.154 = f32[128]{0:T(128)S(1)} all-reduce(f32[128]{0:T(128)S(1)} %get-tuple-element.15), channel_id=1, replica_groups=mesh['blk'=8,'span'=4] {'blk','span'}, use_global_device_ids=true, to_apply=%region_29.30 | all-reduce | flops 128 | bytes 1024 | tf_op jit(solution)/shard_map/psum | solution.py:24
  714.3 5.5 all_gather.45
  736.2 37.7 %psum.155 = f32[128]{0:T(128)S(1)} all-reduce(f32[128]{0:T(128)S(1)} %get-tuple-element.81), channel_id=1, replica_groups=mesh['blk'=8,'span'=4] {'blk','span'}, use_global_device_ids=true, to_apply=%region_31.32 | all-reduce | flops 128 | bytes 1024 | tf_op jit(solution)/shard_map/psum | solution.py:94
  773.9 41.2 %psum.156 = f32[128]{0:T(128)S(1)} all-reduce(f32[128]{0:T(128)S(1)} %get-tuple-element.13), channel_id=1, replica_groups=mesh['blk'=8,'span'=4] {'blk','span'}, use_global_device_ids=true, to_apply=%region_33.34 | all-reduce | flops 128 | bytes 1024 | tf_op jit(solution)/shard_map/psum | solution.py:24
  815.1 5.5 all_gather.46
  837.0 37.7 %psum.157 = f32[128]{0:T(128)S(1)} all-reduce(f32[128]{0:T(128)S(1)} %get-tuple-element.83), channel_id=1, replica_groups=mesh['blk'=8,'span'=4] {'blk','span'}, use_global_device_ids=true, to_apply=%region_35.36 | all-reduce | flops 128 | bytes 1024 | tf_op jit(solution)/shard_map/psum | solution.py:94
  874.8 41.2 %psum.158 = f32[128]{0:T(128)S(1)} all-reduce(f32[128]{0:T(128)S(1)} %multiply_reduce_fusion), channel_id=1, replica_groups=mesh['blk'=8,'span'=4] {'blk','span'}, use_global_device_ids=true, to_apply=%region_37.38 | all-reduce | flops 128 | bytes 1024 | tf_op jit(solution)/shard_map/psum | solution.py:24
  915.9 5.8 all_gather.47
  938.0 37.8 %psum.159 = f32[128]{0:T(128)S(1)} all-reduce(f32[128]{0:T(128)S(1)} %fusion.49), channel_id=1, replica_groups=mesh['blk'=8,'span'=4] {'blk','span'}, use_global_device_ids=true, to_apply=%region_39.40 | all-reduce | flops 128 | bytes 1024 | tf_op jit(solution)/shard_map/psum | solution.py:94
  (275 shorter events, 191.1 us)
Async XLA Ops:
  1.3 12.2 %collective-permute-start = (s32[32]{0:T(128)S(1)}, s32[32]{0:T(128)S(1)}, u32[]{:S(2)}, u32[]{:S(2)}) collective-permute-start(s32[32]{0:T(128)S(1)} %bitcast.731), channel_id=1, source_target_pairs={{28,0},{0,4},{4,8},{8,12},{12,16},{16,20},{20,24},{24,28},{29,1},{... | collective-permute-start | bytes 392 | tf_op jit(solution)/shard_map/ppermute | solution.py:20
  4.3 14.9 %collective-permute-start.4 = (s32[32]{0:T(128)}, s32[32]{0:T(128)S(1)}, u32[]{:S(2)}, u32[]{:S(2)}) collective-permute-start(s32[32]{0:T(128)} %bitcast.732), channel_id=1, source_target_pairs={{28,0},{0,4},{4,8},{8,12},{12,16},{16,20},{20,24},{24,28},{29,1},{... | collective-permute-start | bytes 392 | tf_op jit(solution)/shard_map/ppermute | solution.py:20
  19.2 6.7 collective-permute-start.1
  20.7 6.7 collective-permute-start.5
  40.5 6.7 collective-permute-start.6
  42.0 6.7 collective-permute-start.9
  137.9 4.7 collective-permute-start.12
  141.2 6.7 collective-permute-start.10
  142.7 6.7 collective-permute-start.13
  238.7 4.7 collective-permute-start.16
  242.0 6.7 collective-permute-start.14
  243.5 6.7 collective-permute-start.17
  342.9 6.7 collective-permute-start.18
  344.4 6.7 collective-permute-start.21
  443.6 6.7 collective-permute-start.22
  445.1 6.7 collective-permute-start.25
  503.0 6.7 collective-permute-start.26
  504.5 6.7 collective-permute-start.29
  523.7 6.7 collective-permute-start.30
  525.2 6.7 collective-permute-start.33
  620.9 5.2 collective-permute-start.36
  624.6 6.7 collective-permute-start.34
  626.2 6.7 collective-permute-start.37
  721.6 5.2 collective-permute-start.40
  725.4 6.7 collective-permute-start.38
  726.9 6.7 collective-permute-start.41
  822.4 5.1 collective-permute-start.44
  826.1 6.7 collective-permute-start.42
  827.6 6.7 collective-permute-start.45
  923.5 5.1 collective-permute-start.48
  927.1 6.7 collective-permute-start.46
  928.6 6.7 collective-permute-start.49
  (28 other events, 144.6 us)
where the time goes:
time: 989 us; the launch traced here: 977 us
  blocking collectives  774 us (78%)
  waiting for transfers between devices  107 us (11%)
  starting transfers between devices  63.3 us (6%)
  local copies, waits for them, and re-layouts  21.7 us (2%)
    psum x10, blocking collectives, column_norm(): return lax.psum(jnp.sum(vector * vector, axis=(0, 1)), ('blk', 'span'))  405 us
    psum x8, blocking collectives, shards(): curve = lax.psum(jnp.sum(direction * image, axis=(0, 1)), ('blk', 'span'))  303 us
    ppermute x50, waiting for transfers between devices, passed_along(): return lax.ppermute(block, axis, route)  107 us
    all_gather x12, blocking collectives, stiff_op(): gathered = lax.all_gather(vector, 'span', axis=1, tiled=True)  65.5 us
    ppermute x50, starting transfers between devices, passed_along(): return lax.ppermute(block, axis, route)  63.3 us
  transfers between devices with their start and end apart: 50, of which 48 were waited for; matrix products, arithmetic and copies ran while one was open for 1% of the time, Pallas kernels for 0%

commit v1 on v0

--- a/solution.py
+++ b/solution.py
@@ -1,6 +1,10 @@
+import functools
+
 import jax
 import jax.numpy as jnp
 from jax import lax
+from jax.experimental import pallas as pl
+from jax.experimental.pallas import tpu as pltpu
 from jax.sharding import PartitionSpec as P
 
 BND = 64
@@ -12,6 +16,12 @@
 stick_rate = 20.0
 slip_rate = 0.5
 cycle_rate = 4.0
+
+MESH = pl.DeviceIdType.MESH
+LANES = 128
+SUB = 8
+CASES = 4
+f32, bf16 = jnp.float32, jnp.bfloat16
 
 
 def passed_along(block, axis, distance):
@@ -104,6 +114,361 @@
     return (displacement, velocity, acceleration)
 
 
+def lanes_dot(a, b):
+    return lax.dot_general(a, b, (((1,), (1,)), ((), ())), preferred_element_type=f32)
+
+
+def two_parts(x):
+    high = x.astype(bf16).astype(f32)
+    return high, x - high
+
+
+def swap_halves(tile):
+    return pltpu.roll(tile, CASES, 0)
+
+
+def wheel_kernel(
+    blks,
+    spans,
+    cls_ref,
+    kst_ref,
+    tab_ref,
+    mass_ref,
+    near_ref,
+    far_ref,
+    state_ref,
+    disp_ref,
+    vel_ref,
+    acc_ref,
+    load_ref,
+    disp_out,
+    vel_out,
+    acc_out,
+    send,
+    recv,
+    kfull,
+    back_send,
+    back_recv,
+    onehot_near,
+    onehot_far,
+    weights,
+    kweights,
+    mass_s,
+    diag_s,
+    turned,
+    send_sem,
+    recv_sem,
+    ksend_sem,
+    krecv_sem,
+    bsend_sem,
+    brecv_sem,
+):
+    count = blks * spans
+    blk, span = lax.axis_index("blk"), lax.axis_index("span")
+    me = blk * spans + span
+    rows = kst_ref.shape[0]
+    width = kst_ref.shape[1]
+
+    def other(k):
+        there = lax.rem(me + k, count)
+        return there, (there // spans, lax.rem(there, spans))
+
+    barrier = pltpu.get_barrier_semaphore()
+    for k in range(1, count):
+        pl.semaphore_signal(barrier, inc=1, device_id=other(k)[1], device_id_type=MESH)
+
+    row = lax.broadcasted_iota(jnp.int32, (SUB, LANES), 0)
+    lane = lax.broadcasted_iota(jnp.int32, (SUB, LANES), 1)
+    mine = (lane // rows) == span
+    low = row < CASES
+
+    class_row = lax.broadcasted_iota(jnp.int32, tab_ref.shape, 0)
+    extra = jnp.sum(jnp.where(class_row == cls_ref[0], tab_ref[...], 0.0), axis=0, keepdims=True)
+    mass_here = mass_ref[...]
+    rate = jnp.where(state_ref[...] == 1, 0.25 * stick_rate, 0.25 * slip_rate).astype(f32)
+    contact = jnp.concatenate([near_ref[...].astype(f32), far_ref[...].astype(f32), rate, rate], 1)
+    wide_mass = jnp.where(mine, jnp.concatenate([mass_here] * spans, 1), 0.0)
+    wide_extra = jnp.where(mine, jnp.concatenate([0.25 * extra] * spans, 1), 0.0)
+    constants = jnp.where(
+        row == CASES, wide_mass, jnp.where(row == CASES + 1, wide_extra, jnp.broadcast_to(contact, (SUB, LANES)))
+    )
+
+    disp, vel, acc = disp_ref[0], vel_ref[0], acc_ref[0]
+    mass_col = jnp.sum(
+        jnp.where(
+            lax.broadcasted_iota(jnp.int32, (rows, rows), 0) == lax.broadcasted_iota(jnp.int32, (rows, rows), 1),
+            jnp.broadcast_to(mass_here, (rows, rows)),
+            0.0,
+        ),
+        axis=1,
+        keepdims=True,
+    )
+    inertia = mass_col * acc
+    ahead = disp + vel + 0.5 * acc
+    later = ahead + vel + 1.5 * acc
+    stacked = jnp.concatenate([ahead, load_ref[0, 0] - inertia, later, load_ref[1, 0] - inertia], 0)
+    flipped = stacked.T
+    for j in range(count // 2):
+        tile = flipped[SUB * j : SUB * (j + 1)]
+        send[2 * j] = jnp.where(low, tile, constants)
+        send[2 * j + 1] = jnp.where(low, swap_halves(tile), constants)
+
+    pl.semaphore_wait(barrier, count - 1)
+    for k in range(1, spans):
+        pltpu.make_async_remote_copy(
+            src_ref=kst_ref,
+            dst_ref=kfull.at[pl.ds(pl.multiple_of(span * rows, rows), rows)],
+            send_sem=ksend_sem,
+            recv_sem=krecv_sem,
+            device_id=(blk, lax.rem(span + k, spans)),
+            device_id_type=MESH,
+        ).start()
+    for k in range(1, count):
+        there, place = other(k)
+        pltpu.make_async_remote_copy(
+            src_ref=send.at[there],
+            dst_ref=recv.at[me],
+            send_sem=send_sem,
+            recv_sem=recv_sem,
+            device_id=place,
+            device_id_type=MESH,
+        ).start()
+    recv[me] = send[me]
+    kfull[pl.ds(pl.multiple_of(span * rows, rows), rows), :] = kst_ref[...]
+
+    rest = pl.ds(0, (spans - 1) * rows)
+    pltpu.make_async_copy(kfull.at[rest], kfull.at[rest], krecv_sem).wait()
+    kscaled = 0.25 * kfull[...]
+    khigh, klow = two_parts(kscaled)
+    kweights[:, :width] = khigh.astype(bf16)
+    kweights[:, width:] = klow.astype(bf16)
+
+    others = pl.ds(0, count - 1)
+    pltpu.make_async_copy(recv.at[others], recv.at[others], recv_sem).wait()
+
+    sub_index = lax.broadcasted_iota(jnp.int32, (width, LANES), 0).astype(f32)
+    face_lane = lax.broadcasted_iota(jnp.int32, (1, LANES), 1) < near_ref.shape[1]
+    ones = jnp.ones((2 * SUB, LANES), bf16)
+    near_diag, far_diag, own = [], [], []
+    for b in range(blks):
+        tiles = [recv[b * spans + s] for s in range(spans)]
+        total = tiles[0]
+        for tile in tiles[1:]:
+            total = total + tile
+        own.append((total[CASES : CASES + 1], total[CASES + 1 : CASES + 2]))
+        faces = tiles[0][CASES + 2 : CASES + 3]
+        near_row = faces
+        far_row = pltpu.roll(faces, LANES - near_ref.shape[1], 1)
+        rate_row = jnp.where(face_lane, pltpu.roll(faces, LANES - 2 * near_ref.shape[1], 1), 0.0)
+        near_hot = jnp.where(sub_index == near_row, rate_row, 0.0).astype(bf16)
+        far_hot = jnp.where((sub_index == far_row) & face_lane, 1.0, 0.0).astype(bf16)
+        onehot_near[b] = near_hot
+        onehot_far[b] = far_hot
+        near_diag.append(lanes_dot(ones, near_hot))
+        far_diag.append(lanes_dot(jnp.broadcast_to(rate_row, (2 * SUB, LANES)).astype(bf16), far_hot))
+
+    n_row = lax.broadcasted_iota(jnp.int32, (width, width), 0)
+    n_col = lax.broadcasted_iota(jnp.int32, (width, width), 1)
+    tie = 0.25 * cycle_rate
+    shift_down = jnp.where((n_row == n_col + (width - BND)) & (n_col < BND), tie, 0.0)
+    shift_up = jnp.where((n_col == n_row + (width - BND)) & (n_row < BND), tie, 0.0)
+    lane_row = lax.broadcasted_iota(jnp.int32, (1, LANES), 1)
+    ends = jnp.where(lane_row < BND, tie, 0.0) + jnp.where(lane_row >= width - BND, tie, 0.0)
+    for b in range(blks):
+        prev = (b - 1) % blks
+        j, half = divmod(b, 2)
+        mass_s[j, CASES * half : CASES * (half + 1), :] = jnp.broadcast_to(own[b][0], (CASES, LANES))
+        diag_row = own[b][1] + ends + near_diag[b][0:1] + far_diag[prev][0:1]
+        diag_s[j, CASES * half : CASES * (half + 1), :] = jnp.broadcast_to(diag_row, (CASES, LANES))
+        before = -(lanes_dot(onehot_near[prev], onehot_far[prev]) + shift_down)
+        after = -(lanes_dot(onehot_far[b], onehot_near[b]) + shift_up)
+        group = j if half == 0 else (j + 1) % (blks // 2)
+        base = 2 * width * half
+        for part, block in enumerate((before, after)):
+            high, small = two_parts(block)
+            weights[group, width * part : width * (part + 1), base : base + width] = high.astype(bf16)
+            weights[group, width * part : width * (part + 1), base + width : base + 2 * width] = small.astype(bf16)
+
+    pairs = blks // 2
+    group_of = lane // rows
+    pieces = [[] for _ in range(4)]
+    for j in range(pairs):
+        parts = [
+            jnp.where(low, recv[2 * j * spans + s], swap_halves(recv[(2 * j + 1) * spans + s])) for s in range(spans)
+        ]
+        for k in range(4):
+            value = None
+            for s in range(spans):
+                turn = (rows * (s - k)) % LANES
+                moved = pltpu.roll(parts[s], turn, 1) if turn else parts[s]
+                value = moved if value is None else jnp.where(group_of == s, moved, value)
+            pieces[k].append(value)
+    u0, force0, u1, force1 = (jnp.stack(p) for p in pieces)
+    mass = mass_s[...]
+    diag = diag_s[...]
+
+    def quarter_k(v):
+        high, small = two_parts(v)
+        both = jnp.concatenate([high.reshape(pairs * SUB, LANES), small.reshape(pairs * SUB, LANES)], 0).astype(bf16)
+        p = jnp.dot(both, kweights[...], preferred_element_type=f32)
+        h = pairs * SUB
+        common = p[:h, :width] + (p[h:, :width] + p[:h, width:])
+        tiles = []
+        for j in range(pairs):
+            t = jnp.concatenate([swap_halves(high[j]), swap_halves(small[j])], 0)
+            tiles.append(t.astype(bf16))
+        across = []
+        for j in range(pairs):
+            lhs = jnp.concatenate([tiles[j - 1], tiles[j]], 1)
+            g = jnp.dot(lhs, weights[j], preferred_element_type=f32)
+            even = g[:SUB, :width] + (g[SUB:, :width] + g[:SUB, width : 2 * width])
+            odd = g[:SUB, 2 * width : 3 * width] + (g[SUB:, 2 * width : 3 * width] + g[:SUB, 3 * width :])
+            across.append((even, odd))
+        sides = jnp.stack([jnp.where(low, across[j][0], across[(j + 1) % pairs][1]) for j in range(pairs)])
+        return diag * v + common.reshape(pairs, SUB, LANES) + sides
+
+    def per_case(v):
+        t = v[0]
+        for j in range(1, pairs):
+            t = t + v[j]
+        t = t + swap_halves(t)
+        return jnp.sum(t, axis=1, keepdims=True)
+
+    def solve(residual):
+        direction = residual
+        gained = jnp.zeros_like(residual)
+        norm_now = per_case(residual * residual)
+        for iteration in range(ITERS):
+            image = mass * direction + quarter_k(direction)
+            step_length = (norm_now / per_case(direction * image))[None]
+            gained = gained + step_length * direction
+            residual = residual - step_length * image
+            if iteration < ITERS - 1:
+                norm_next = per_case(residual * residual)
+                direction = residual + (norm_next / norm_now)[None] * direction
+                norm_now = norm_next
+        return gained, residual
+
+    start0 = force0 - 4.0 * quarter_k(u0)
+    start1 = force1 - 4.0 * quarter_k(u1)
+    gain0, left0 = solve(start0)
+    gain1, _ = solve(start1 - 5.0 * (start0 - left0) + 4.0 * mass * gain0)
+
+    for j in range(pairs):
+        back_send[2 * j] = jnp.where(low, gain0[j], swap_halves(gain1[j]))
+        back_send[2 * j + 1] = jnp.where(low, swap_halves(gain0[j]), gain1[j])
+    for k in range(1, count):
+        there, place = other(k)
+        pltpu.make_async_remote_copy(
+            src_ref=back_send.at[there // spans],
+            dst_ref=back_recv.at[me],
+            send_sem=bsend_sem,
+            recv_sem=brecv_sem,
+            device_id=place,
+            device_id_type=MESH,
+        ).start()
+    back_recv[me] = back_send[blk]
+    pltpu.make_async_copy(kfull.at[rest], kfull.at[rest], ksend_sem).wait()
+    pltpu.make_async_copy(send.at[others], send.at[others], send_sem).wait()
+    pltpu.make_async_copy(back_recv.at[others], back_recv.at[others], brecv_sem).wait()
+
+    first, second = [], []
+    for j in range(count // 2):
+        a, b = back_recv[2 * j], back_recv[2 * j + 1]
+        first.append(jnp.where(low, a, swap_halves(b)))
+        second.append(jnp.where(low, swap_halves(a), b))
+    turned[0] = jnp.concatenate(first, 0).T
+    turned[1] = jnp.concatenate(second, 0).T
+    here = pl.ds(pl.multiple_of(span * rows, rows), rows)
+    g0, g1 = turned[0, here, :], turned[1, here, :]
+    acc1 = acc + g0
+    acc2 = acc1 + g1
+    vel1 = vel + acc + 0.5 * g0
+    disp1 = ahead + 0.25 * g0
+    disp_out[0] = disp1 + vel1 + 0.25 * acc1 + 0.25 * acc2
+    vel_out[0] = vel1 + 0.5 * (acc1 + acc2)
+    acc_out[0] = acc2
+    pltpu.make_async_copy(back_recv.at[others], back_recv.at[others], bsend_sem).wait()
+
+
+def wheel_shards(
+    blks,
+    spans,
+    stiffness,
+    mistune_table,
+    sector_class,
+    lumped_mass,
+    near_faces,
+    far_faces,
+    contact_state,
+    displacement,
+    velocity,
+    acceleration,
+    load_steps,
+):
+    width = stiffness.shape[1]
+    count = blks * spans
+    vmem = pl.BlockSpec(memory_space=pltpu.VMEM)
+    dma = pltpu.SemaphoreType.DMA
+    return pl.pallas_call(
+        functools.partial(wheel_kernel, blks, spans),
+        out_shape=[jax.ShapeDtypeStruct(displacement.shape, f32)] * 3,
+        in_specs=[pl.BlockSpec(memory_space=pltpu.SMEM)] + [vmem] * 10,
+        out_specs=[vmem] * 3,
+        scratch_shapes=[
+            pltpu.VMEM((count, SUB, LANES), f32),
+            pltpu.VMEM((count, SUB, LANES), f32),
+            pltpu.VMEM((width, width), f32),
+            pltpu.VMEM((blks, SUB, LANES), f32),
+            pltpu.VMEM((count, SUB, LANES), f32),
+            pltpu.VMEM((blks, width, LANES), bf16),
+            pltpu.VMEM((blks, width, LANES), bf16),
+            pltpu.VMEM((blks // 2, 2 * width, 4 * width), bf16),
+            pltpu.VMEM((width, 2 * width), bf16),
+            pltpu.VMEM((blks // 2, SUB, LANES), f32),
+            pltpu.VMEM((blks // 2, SUB, LANES), f32),
+            pltpu.VMEM((2, LANES, LANES), f32),
+            dma,
+            dma,
+            dma,
+            dma,
+            dma,
+            dma,
+        ],
+        compiler_params=pltpu.CompilerParams(
+            collective_id=0, has_side_effects=True, vmem_limit_bytes=24 * 1024 * 1024
+        ),
+    )(
+        sector_class,
+        stiffness,
+        mistune_table,
+        lumped_mass,
+        near_faces,
+        far_faces,
+        contact_state,
+        displacement,
+        velocity,
+        acceleration,
+        load_steps,
+    )
+
+
+def one_tile(mesh, stiffness, near_faces, displacement, load_steps):
+    blks, spans = mesh.shape["blk"], mesh.shape["span"]
+    sectors, width, cases = displacement.shape
+    return (
+        sectors == blks
+        and blks % 2 == 0
+        and width == LANES
+        and cases == LANES
+        and cases == CASES * blks * spans
+        and 4 * (width // spans) == LANES
+        and spans == 4
+        and 4 * near_faces.shape[1] == LANES
+        and load_steps.shape[0] == STEPS == 2
+    )
+
+
 def solution(mesh):
     placed = (
         P("span", None),
@@ -118,10 +483,18 @@
         P("blk", "span", None),
         P(None, "blk", "span", None),
     )
-    return jax.shard_map(
-        shards,
-        mesh=mesh,
-        in_specs=placed,
-        out_specs=(P("blk", "span", None), P("blk", "span", None), P("blk", "span", None)),
-        check_vma=False,
-    )
+
+    def run(*arrays):
+        if one_tile(mesh, arrays[0], arrays[4], arrays[7], arrays[10]):
+            body = functools.partial(wheel_shards, mesh.shape["blk"], mesh.shape["span"])
+        else:
+            body = shards
+        return jax.shard_map(
+            body,
+            mesh=mesh,
+            in_specs=placed,
+            out_specs=(P("blk", "span", None), P("blk", "span", None), P("blk", "span", None)),
+            check_vma=False,
+        )(*arrays)
+
+    return run

time: 989 us -> 31.6 us (0.03); the launches traced: 977 us -> 31 us
  blocking collectives: 774 us -> 0 us
  waiting for transfers between devices: 107 us -> 0 us
  starting transfers between devices: 63.3 us -> 0 us
  Pallas kernels: 0 us -> 22.8 us
  local copies, waits for them, and re-layouts: 21.7 us -> 6.79 us
    psum x18 -> x0, blocking collectives: 709 us -> none  [the longest x10 405 us: column_norm(): return lax.psum(jnp.sum(vector * vector, axis=(0, 1)), ('blk', 'span'))]
    ppermute x50 -> x0, waiting for transfers between devices: 107 us -> none  [passed_along(): return lax.ppermute(block, axis, route)]
    all_gather x12 -> x0, blocking collectives: 65.5 us -> none  [stiff_op(): gathered = lax.all_gather(vector, 'span', axis=1, tiled=True)]
    ppermute x50 -> x0, starting transfers between devices: 63.3 us -> none  [passed_along(): return lax.ppermute(block, axis, route)]
    pallas_call x0 -> x1, Pallas kernels: none -> 22.8 us  [wheel_shards(): pl.pallas_call(functools.partial(wheel_kernel, blks, spans), out_shape=[j...]
    gather x13 -> x0, local copies, waits for them, and re-layouts: 19.7 us -> none  [shards(): pick_rows = jax.vmap(lambda values, rows: values[rows])]
  transfers between devices with their start and end apart: 50 -> 0, of which waited for: 48 -> 0; matrix products, arithmetic and copies ran while one was open for 1% -> 0% of each run, Pallas kernels for 0% -> 0%
where the time goes in v1:
time: 31.6 us; the launch traced here: 31 us
  Pallas kernels  22.8 us (72%)
  local copies, waits for them, and re-layouts  6.79 us (21%)
  between operations  1.38 us (4%)
    pallas_call x1, Pallas kernels, wheel_shards(): pl.pallas_call(functools.partial(wheel_kernel, blks, spans), out_shape=[j...  22.8 us
    unnamed x23, local copies, waits for them, and re-layouts  6.79 us

profile of v1, /device:TPU:0, one launch (start us, length us, event | category | flops | bytes accessed | tf_op | source)
XLA Modules:
  0.0 31.0 jit_solution(2801431715444263129)
XLA Ops:
  0.6 0.0 copy-start.8
  0.6 0.0 copy-start.7
  0.7 0.0 copy-start.6
  1.3 0.0 copy-done.8
  1.3 0.0 copy-done.7
  1.4 0.0 copy-done.6
  1.4 0.0 copy-start
  1.4 0.7 %copy-done = f32[2,1,32,128]{3,2,1,0:T(8,128)S(1)} copy-done((f32[2,1,32,128]{3,2,1,0:T(8,128)S(1)}, f32[2,1,32,128]{3,2,1,0:T(8,128)}, u32[]{:S(2)}) %copy-start) | copy-done | bytes 32792
  2.1 0.0 copy-start.1
  2.1 0.7 %copy-done.1 = f32[32,128]{1,0:T(8,128)S(1)} copy-done((f32[32,128]{1,0:T(8,128)S(1)}, f32[32,128]{1,0:T(8,128)}, u32[]{:S(2)}) %copy-start.1) | copy-done | bytes 16408
  2.8 0.0 copy-start.2
  2.8 0.7 %copy-done.2 = f32[1,32,128]{2,1,0:T(8,128)S(1)} copy-done((f32[1,32,128]{2,1,0:T(8,128)S(1)}, f32[1,32,128]{2,1,0:T(8,128)}, u32[]{:S(2)}) %copy-start.2) | copy-done | bytes 16408
  3.6 0.0 copy-start.3
  3.6 0.7 %copy-done.3 = f32[1,32,128]{2,1,0:T(8,128)S(1)} copy-done((f32[1,32,128]{2,1,0:T(8,128)S(1)}, f32[1,32,128]{2,1,0:T(8,128)}, u32[]{:S(2)}) %copy-start.3) | copy-done | bytes 16408
  4.3 0.0 copy-start.4
  4.3 0.7 %copy-done.4 = f32[1,32,128]{2,1,0:T(8,128)S(1)} copy-done((f32[1,32,128]{2,1,0:T(8,128)S(1)}, f32[1,32,128]{2,1,0:T(8,128)}, u32[]{:S(2)}) %copy-start.4) | copy-done | bytes 16408
  5.0 0.0 copy-start.5
  5.0 0.7 %copy-done.5 = f32[8,32]{1,0:T(8,128)S(1)} copy-done((f32[8,32]{1,0:T(8,128)S(1)}, f32[8,32]{1,0:T(8,128)}, u32[]{:S(2)}) %copy-start.5) | copy-done | bytes 1048
  5.7 0.0 copy-start.9
  5.7 0.7 %copy-done.9 = s32[1,32]{1,0:T(1,128)S(1)} copy-done((s32[1,32]{1,0:T(1,128)S(1)}, s32[1,32]{1,0:T(1,128)}, u32[]{:S(2)}) %copy-start.9) | copy-done | bytes 152
  6.3 22.8 %shard_map.130 = (f32[1,32,128]{2,1,0:T(8,128)S(1)}, f32[1,32,128]{2,1,0:T(8,128)S(1)}, f32[1,32,128]{2,1,0:T(8,128)S(1)}) custom-call(s32[1]{0:T(128)S(6)} %copy.17.cls_ref, f32[32,128]{1,0:T(8,128)S(1)} %copy-done.1, f32[8,32]{1,0:T(8,128)S(1)} %copy-done.5, f32[1,32]{1,0:T(1,128)S(1)} %copy-done.6, s32[1,32]{1,0:T(1,128)S(1)} %copy-done.7, ...), custom_call_target="tpu_custom_call" | custom-call | tf_op jit(solution)/shard_map/pallas_call | solution.py:413
  29.2 0.6 %copy.18 = f32[1,32,128]{2,1,0:T(8,128)} copy(f32[1,32,128]{2,1,0:T(8,128)S(1)} %get-tuple-element.6) | data formatting | bytes 32768
  29.8 0.6 %copy.19 = f32[1,32,128]{2,1,0:T(8,128)} copy(f32[1,32,128]{2,1,0:T(8,128)S(1)} %get-tuple-element.7) | data formatting | bytes 32768
  30.4 0.6 %copy.20 = f32[1,32,128]{2,1,0:T(8,128)} copy(f32[1,32,128]{2,1,0:T(8,128)S(1)} %get-tuple-element.8) | data formatting | bytes 32768
Async XLA Ops:
  0.6 0.7 %copy-start.8 = (s32[1,32]{1,0:T(1,128)S(1)}, s32[1,32]{1,0:T(1,128)}, u32[]{:S(2)}) copy-start(s32[1,32]{1,0:T(1,128)} %far_ref.1) | copy-start | bytes 388
  0.6 0.7 %copy-start.7 = (s32[1,32]{1,0:T(1,128)S(1)}, s32[1,32]{1,0:T(1,128)}, u32[]{:S(2)}) copy-start(s32[1,32]{1,0:T(1,128)} %near_ref.1) | copy-start | bytes 388
  0.7 0.7 %copy-start.6 = (f32[1,32]{1,0:T(1,128)S(1)}, f32[1,32]{1,0:T(1,128)}, u32[]{:S(2)}) copy-start(f32[1,32]{1,0:T(1,128)} %mass_ref.1) | copy-start | bytes 388
  1.4 0.8 %copy-start = (f32[2,1,32,128]{3,2,1,0:T(8,128)S(1)}, f32[2,1,32,128]{3,2,1,0:T(8,128)}, u32[]{:S(2)}) copy-start(f32[2,1,32,128]{3,2,1,0:T(8,128)} %load_ref.1) | copy-start | bytes 98308
  2.1 0.7 %copy-start.1 = (f32[32,128]{1,0:T(8,128)S(1)}, f32[32,128]{1,0:T(8,128)}, u32[]{:S(2)}) copy-start(f32[32,128]{1,0:T(8,128)} %kst_ref.1) | copy-start | bytes 49156
  2.8 0.7 %copy-start.2 = (f32[1,32,128]{2,1,0:T(8,128)S(1)}, f32[1,32,128]{2,1,0:T(8,128)}, u32[]{:S(2)}) copy-start(f32[1,32,128]{2,1,0:T(8,128)} %disp_ref.1) | copy-start | bytes 49156
  3.6 0.7 %copy-start.3 = (f32[1,32,128]{2,1,0:T(8,128)S(1)}, f32[1,32,128]{2,1,0:T(8,128)}, u32[]{:S(2)}) copy-start(f32[1,32,128]{2,1,0:T(8,128)} %vel_ref.1) | copy-start | bytes 49156
  4.3 0.7 %copy-start.4 = (f32[1,32,128]{2,1,0:T(8,128)S(1)}, f32[1,32,128]{2,1,0:T(8,128)}, u32[]{:S(2)}) copy-start(f32[1,32,128]{2,1,0:T(8,128)} %acc_ref.1) | copy-start | bytes 49156
  5.0 0.7 %copy-start.5 = (f32[8,32]{1,0:T(8,128)S(1)}, f32[8,32]{1,0:T(8,128)}, u32[]{:S(2)}) copy-start(f32[8,32]{1,0:T(8,128)} %tab_ref.1) | copy-start | bytes 3076
  5.7 0.7 %copy-start.9 = (s32[1,32]{1,0:T(1,128)S(1)}, s32[1,32]{1,0:T(1,128)}, u32[]{:S(2)}) copy-start(s32[1,32]{1,0:T(1,128)} %state_ref.1) | copy-start | bytes 388

commit v2 on v1

--- a/solution.py
+++ b/solution.py
@@ -130,17 +130,17 @@
 def wheel_kernel(
     blks,
     spans,
-    cls_ref,
-    kst_ref,
-    tab_ref,
-    mass_ref,
-    near_ref,
-    far_ref,
-    state_ref,
-    disp_ref,
-    vel_ref,
-    acc_ref,
-    load_ref,
+    cls_hbm,
+    kst_hbm,
+    tab_hbm,
+    mass_hbm,
+    near_hbm,
+    far_hbm,
+    state_hbm,
+    disp_hbm,
+    vel_hbm,
+    acc_hbm,
+    load_hbm,
     disp_out,
     vel_out,
     acc_out,
@@ -156,6 +156,18 @@
     mass_s,
     diag_s,
     turned,
+    cls_ref,
+    kst_ref,
+    tab_ref,
+    mass_ref,
+    near_ref,
+    far_ref,
+    state_ref,
+    disp_ref,
+    vel_ref,
+    acc_ref,
+    load_ref,
+    in_sem,
     send_sem,
     recv_sem,
     ksend_sem,
@@ -169,6 +181,27 @@
     rows = kst_ref.shape[0]
     width = kst_ref.shape[1]
 
+    moves = [
+        pltpu.make_async_copy(source, target, in_sem.at[i])
+        for i, (source, target) in enumerate(
+            (
+                (disp_hbm, disp_ref),
+                (vel_hbm, vel_ref),
+                (acc_hbm, acc_ref),
+                (load_hbm, load_ref),
+                (mass_hbm, mass_ref),
+                (cls_hbm, cls_ref),
+                (tab_hbm, tab_ref),
+                (near_hbm, near_ref),
+                (far_hbm, far_ref),
+                (state_hbm, state_ref),
+                (kst_hbm, kst_ref),
+            )
+        )
+    ]
+    for move in moves:
+        move.start()
+
     def other(k):
         there = lax.rem(me + k, count)
         return there, (there // spans, lax.rem(there, spans))
@@ -176,6 +209,9 @@
     barrier = pltpu.get_barrier_semaphore()
     for k in range(1, count):
         pl.semaphore_signal(barrier, inc=1, device_id=other(k)[1], device_id_type=MESH)
+
+    for move in moves:
+        move.wait()
 
     row = lax.broadcasted_iota(jnp.int32, (SUB, LANES), 0)
     lane = lax.broadcasted_iota(jnp.int32, (SUB, LANES), 1)
@@ -391,6 +427,17 @@
     pltpu.make_async_copy(back_recv.at[others], back_recv.at[others], bsend_sem).wait()
 
 
+def hand_over(a_in, b_in, c_in, a_out, b_out, c_out, sem):
+    moves = [
+        pltpu.make_async_copy(source, target, sem.at[i])
+        for i, (source, target) in enumerate(((a_in, a_out), (b_in, b_out), (c_in, c_out)))
+    ]
+    for move in moves:
+        move.start()
+    for move in moves:
+        move.wait()
+
+
 def wheel_shards(
     blks,
     spans,
@@ -408,12 +455,25 @@
 ):
     width = stiffness.shape[1]
     count = blks * spans
+    operands = (
+        sector_class,
+        stiffness,
+        mistune_table,
+        lumped_mass,
+        near_faces,
+        far_faces,
+        contact_state,
+        displacement,
+        velocity,
+        acceleration,
+        load_steps,
+    )
     vmem = pl.BlockSpec(memory_space=pltpu.VMEM)
     dma = pltpu.SemaphoreType.DMA
-    return pl.pallas_call(
+    results = pl.pallas_call(
         functools.partial(wheel_kernel, blks, spans),
         out_shape=[jax.ShapeDtypeStruct(displacement.shape, f32)] * 3,
-        in_specs=[pl.BlockSpec(memory_space=pltpu.SMEM)] + [vmem] * 10,
+        in_specs=[pl.BlockSpec(memory_space=pltpu.HBM)] * 11,
         out_specs=[vmem] * 3,
         scratch_shapes=[
             pltpu.VMEM((count, SUB, LANES), f32),
@@ -428,6 +488,9 @@
             pltpu.VMEM((blks // 2, SUB, LANES), f32),
             pltpu.VMEM((blks // 2, SUB, LANES), f32),
             pltpu.VMEM((2, LANES, LANES), f32),
+            pltpu.SMEM(sector_class.shape, jnp.int32),
+            *(pltpu.VMEM(a.shape, a.dtype) for a in operands[1:]),
+            pltpu.SemaphoreType.DMA((len(operands),)),
             dma,
             dma,
             dma,
@@ -436,21 +499,16 @@
             dma,
         ],
         compiler_params=pltpu.CompilerParams(
-            collective_id=0, has_side_effects=True, vmem_limit_bytes=24 * 1024 * 1024
+            collective_id=0, has_side_effects=True
         ),
-    )(
-        sector_class,
-        stiffness,
-        mistune_table,
-        lumped_mass,
-        near_faces,
-        far_faces,
-        contact_state,
-        displacement,
-        velocity,
-        acceleration,
-        load_steps,
-    )
+    )(*operands)
+    return pl.pallas_call(
+        hand_over,
+        out_shape=[jax.ShapeDtypeStruct(displacement.shape, f32)] * 3,
+        in_specs=[pl.BlockSpec(memory_space=pl.ANY)] * 3,
+        out_specs=[pl.BlockSpec(memory_space=pltpu.HBM)] * 3,
+        scratch_shapes=[pltpu.SemaphoreType.DMA((3,))],
+    )(*results)
 
 
 def one_tile(mesh, stiffness, near_faces, displacement, load_steps):

time: 31.6 us -> 27.7 us (0.88); the launches traced: 31 us -> 27.5 us
  local copies, waits for them, and re-layouts: 6.79 us -> 0 us
  Pallas kernels: 22.8 us -> 26.2 us
    unnamed x23 -> x0, local copies, waits for them, and re-layouts: 6.79 us -> none
    pallas_call x0 -> x1, Pallas kernels: none -> 2.62 us  [wheel_shards(): pl.pallas_call(hand_over, out_shape=[jax.ShapeDtypeStruct(displacement.sh...]
    pallas_call x1, Pallas kernels: 22.8 us -> 23.6 us  [wheel_shards(): pl.pallas_call(functools.partial(wheel_kernel, blks, spans), out_shape=[j...]
where the time goes in v2:
time: 27.7 us; the launch traced here: 27.5 us
  Pallas kernels  26.2 us (95%)
  between operations  1.29 us (5%)
    pallas_call x1, Pallas kernels, wheel_shards(): pl.pallas_call(functools.partial(wheel_kernel, blks, spans), out_shape=[j...  23.6 us
    pallas_call x1, Pallas kernels, wheel_shards(): pl.pallas_call(hand_over, out_shape=[jax.ShapeDtypeStruct(displacement.sh...  2.62 us

profile of v2, /device:TPU:0, one launch (start us, length us, event | category | flops | bytes accessed | tf_op | source)
XLA Modules:
  0.0 27.5 jit_solution(3383545132836699295)
XLA Ops:
  1.3 23.6 %shard_map.130 = (f32[1,32,128]{2,1,0:T(8,128)}, f32[1,32,128]{2,1,0:T(8,128)}, f32[1,32,128]{2,1,0:T(8,128)}) custom-call(s32[1]{0:T(128)S(6)} %copy.14.cls_hbm, f32[32,128]{1,0:T(8,128)} %kst_hbm.1, f32[8,32]{1,0:T(8,128)} %tab_hbm.1, f32[1,32]{1,0:T(1,128)} %mass_hbm.1, s32[1,32]{1,0:T(1,128)} %near_hbm.1, s32[1,32]{1,0:T(1,128)} %far_hbm.1, ...), custom_call_target="tpu_custom_call" | custom-call | tf_op jit(solution)/shard_map/pallas_call | solution.py:473
  24.9 2.6 %shard_map.131 = (f32[1,32,128]{2,1,0:T(8,128)}, f32[1,32,128]{2,1,0:T(8,128)}, f32[1,32,128]{2,1,0:T(8,128)}) custom-call(f32[1,32,128]{2,1,0:T(8,128)} %get-tuple-element.6.a_in, f32[1,32,128]{2,1,0:T(8,128)} %get-tuple-element.7.b_in, f32[1,32,128]{2,1,0:T(8,128)} %get-tuple-element.8.c_in), custom_call_target="tpu_custom_call" | custom-call | tf_op jit(solution)/shard_map/pallas_call | solution.py:505

commit v3 on v2

--- a/solution.py
+++ b/solution.py
@@ -141,9 +141,8 @@
     vel_hbm,
     acc_hbm,
     load_hbm,
-    disp_out,
-    vel_out,
-    acc_out,
+    first_out,
+    second_out,
     send,
     recv,
     kfull,
@@ -416,26 +415,9 @@
     turned[0] = jnp.concatenate(first, 0).T
     turned[1] = jnp.concatenate(second, 0).T
     here = pl.ds(pl.multiple_of(span * rows, rows), rows)
-    g0, g1 = turned[0, here, :], turned[1, here, :]
-    acc1 = acc + g0
-    acc2 = acc1 + g1
-    vel1 = vel + acc + 0.5 * g0
-    disp1 = ahead + 0.25 * g0
-    disp_out[0] = disp1 + vel1 + 0.25 * acc1 + 0.25 * acc2
-    vel_out[0] = vel1 + 0.5 * (acc1 + acc2)
-    acc_out[0] = acc2
+    first_out[0] = turned[0, here, :]
+    second_out[0] = turned[1, here, :]
     pltpu.make_async_copy(back_recv.at[others], back_recv.at[others], bsend_sem).wait()
-
-
-def hand_over(a_in, b_in, c_in, a_out, b_out, c_out, sem):
-    moves = [
-        pltpu.make_async_copy(source, target, sem.at[i])
-        for i, (source, target) in enumerate(((a_in, a_out), (b_in, b_out), (c_in, c_out)))
-    ]
-    for move in moves:
-        move.start()
-    for move in moves:
-        move.wait()
 
 
 def wheel_shards(
@@ -472,9 +454,9 @@
     dma = pltpu.SemaphoreType.DMA
     results = pl.pallas_call(
         functools.partial(wheel_kernel, blks, spans),
-        out_shape=[jax.ShapeDtypeStruct(displacement.shape, f32)] * 3,
+        out_shape=[jax.ShapeDtypeStruct(displacement.shape, f32)] * 2,
         in_specs=[pl.BlockSpec(memory_space=pltpu.HBM)] * 11,
-        out_specs=[vmem] * 3,
+        out_specs=[vmem] * 2,
         scratch_shapes=[
             pltpu.VMEM((count, SUB, LANES), f32),
             pltpu.VMEM((count, SUB, LANES), f32),
@@ -502,13 +484,16 @@
             collective_id=0, has_side_effects=True
         ),
     )(*operands)
-    return pl.pallas_call(
-        hand_over,
-        out_shape=[jax.ShapeDtypeStruct(displacement.shape, f32)] * 3,
-        in_specs=[pl.BlockSpec(memory_space=pl.ANY)] * 3,
-        out_specs=[pl.BlockSpec(memory_space=pltpu.HBM)] * 3,
-        scratch_shapes=[pltpu.SemaphoreType.DMA((3,))],
-    )(*results)
+    first, second = results
+    acc1 = acceleration + first
+    acc2 = acc1 + second
+    vel1 = velocity + acceleration + 0.5 * first
+    disp1 = displacement + velocity + 0.5 * acceleration + 0.25 * first
+    return (
+        disp1 + vel1 + 0.25 * acc1 + 0.25 * acc2,
+        vel1 + 0.5 * (acc1 + acc2),
+        acc2,
+    )
 
 
 def one_tile(mesh, stiffness, near_faces, displacement, load_steps):

time: 27.7 us -> 27.2 us (0.982)
  Pallas kernels: 26.2 us -> 23.6 us
  other arithmetic: 0 us -> 2.02 us
    pallas_call x1 -> x0, Pallas kernels: 2.62 us -> none  [wheel_shards(): pl.pallas_call(hand_over, out_shape=[jax.ShapeDtypeStruct(displacement.sh...]
    add x0 -> x2, other arithmetic: none -> 2.02 us  [the longest x1 1.4 us: wheel_shards(): vel1 + 0.5 * (acc1 + acc2)]
where the time goes in v3:
time: 27.2 us; the launch traced here: 26.9 us
  Pallas kernels  23.6 us (87%)
  other arithmetic  2.02 us (7%)
  between operations  1.34 us (5%)
    pallas_call x1, Pallas kernels, wheel_shards(): pl.pallas_call(functools.partial(wheel_kernel, blks, spans), out_shape=[j...  23.6 us
    add x1, other arithmetic, wheel_shards(): vel1 + 0.5 * (acc1 + acc2)  1.4 us
    add x1, other arithmetic, wheel_shards(): disp1 + vel1 + 0.25 * acc1 + 0.25 * acc2  0.62 us

profile of v3, /device:TPU:0, one launch (start us, length us, event | category | flops | bytes accessed | tf_op | source)
XLA Modules:
  0.0 26.9 jit_solution(116555709429662429)
XLA Ops:
  1.3 0.0 copy-start
  1.3 0.0 copy-start.1
  1.3 23.6 %shard_map.130 = (f32[1,32,128]{2,1,0:T(8,128)}, f32[1,32,128]{2,1,0:T(8,128)}) custom-call(s32[1]{0:T(128)S(6)} %copy.14.cls_hbm, f32[32,128]{1,0:T(8,128)} %kst_hbm.1, f32[8,32]{1,0:T(8,128)} %tab_hbm.1, f32[1,32]{1,0:T(1,128)} %mass_hbm.1, s32[1,32]{1,0:T(1,128)} %near_hbm.1, s32[1,32]{1,0:T(1,128)} %far_hbm.1, s32[1,32]{1,0:T(1,128)} %state_hbm.1, ...), custom_call_target="tpu_custom_call" | custom-call | tf_op jit(solution)/shard_map/pallas_call | solution.py:455
  24.9 0.0 copy-done
  24.9 0.0 copy-done.1
  24.9 0.0 copy-start.2
  24.9 0.0 copy-start.4
  24.9 1.4 %multiply_add_fusion = (f32[1,32,128]{2,1,0:T(8,128)}, f32[1,32,128]{2,1,0:T(8,128)S(1)}, f32[1,32,128]{2,1,0:T(8,128)S(1)}) fusion(f32[1,32,128]{2,1,0:T(8,128)} %get-tuple-element.5, f32[1,32,128]{2,1,0:T(8,128)S(1)} %copy-done, f32[1,32,128]{2,1,0:T(8,128)S(1)} %copy-done.1, f32[1,32,128]{2,1,0:T(8,128)} %get-tuple-element.6), kind=kLoop, calls=%fused_computation | loop fusion | flops 32768 | bytes 114688 | tf_op jit(solution)/shard_map/add | solution.py:494
  26.3 0.0 copy-start.3
  26.3 0.0 copy-done.2
  26.3 0.0 copy-done.4
  26.3 0.6 %multiply_add_fusion.1 = f32[1,32,128]{2,1,0:T(8,128)} fusion(f32[1,32,128]{2,1,0:T(8,128)S(1)} %get-tuple-element.8, f32[1,32,128]{2,1,0:T(8,128)S(1)} %get-tuple-element.9, f32[1,32,128]{2,1,0:T(8,128)S(1)} %copy-done.4, f32[1,32,128]{2,1,0:T(8,128)S(1)} %copy-done.1, f32[1,32,128]{2,1,0:T(8,128)S(1)} %copy-done.2, f32[1,32,128]{2,1,0:T(8,128)S(1)} %copy-done), kind=kLoop, calls=%fused_computation.1 | loop fusion | flops 53248 | bytes 114688 | tf_op jit(solution)/shard_map/add | solution.py:493
  26.9 0.0 copy-done.3
Async XLA Ops:
  1.3 23.6 %copy-start = (f32[1,32,128]{2,1,0:T(8,128)S(1)}, f32[1,32,128]{2,1,0:T(8,128)}, u32[]{:S(2)}) copy-start(f32[1,32,128]{2,1,0:T(8,128)} %vel_hbm.1) | copy-start | bytes 49156
  1.3 23.6 %copy-start.1 = (f32[1,32,128]{2,1,0:T(8,128)S(1)}, f32[1,32,128]{2,1,0:T(8,128)}, u32[]{:S(2)}) copy-start(f32[1,32,128]{2,1,0:T(8,128)} %acc_hbm.1) | copy-start | bytes 49156
  24.9 1.4 %copy-start.2 = (f32[1,32,128]{2,1,0:T(8,128)S(1)}, f32[1,32,128]{2,1,0:T(8,128)}, u32[]{:S(2)}) copy-start(f32[1,32,128]{2,1,0:T(8,128)} %disp_hbm.1) | copy-start | bytes 49156
  24.9 1.4 %copy-start.4 = (f32[1,32,128]{2,1,0:T(8,128)S(1)}, f32[1,32,128]{2,1,0:T(8,128)}, u32[]{:S(2)}) copy-start(f32[1,32,128]{2,1,0:T(8,128)} %get-tuple-element.5) | copy-start | bytes 49156
  26.3 0.6 %copy-start.3 = (f32[1,32,128]{2,1,0:T(8,128)}, f32[1,32,128]{2,1,0:T(8,128)S(1)}, u32[]{:S(2)}) copy-start(f32[1,32,128]{2,1,0:T(8,128)S(1)} %get-tuple-element.8) | copy-start | bytes 49156
